TPU v7x, 32 devices: a whole 2x2x4 slice. The times are simulated.
32 devices in a mesh: req: 16 (over z, y, core), tp: 2 (over x).
Axes of the slice: x: 2, y: 2, z: 4, core: 2. Of those that a mesh axis runs over, the one named last changes fastest.
Arguments:
- tokens: bfloat16 [8192, 1024], P(('req', 'tp')), may hold values from -6 to 6
- w_qkv: bfloat16 [1024, 3, 1024], P(None, None, 'tp'), may hold values from -0.1875 to 0.1875
- w_out: bfloat16 [1024, 1024], P('tp'), may hold values from -0.75 to 0.75
- w_up: bfloat16 [1024, 4096], P(None, 'tp'), may hold values from -0.1875 to 0.1875
- b_up: float32 [4096], P('tp'), may hold values from -4 to 4
- w_down: bfloat16 [4096, 1024], P('tp'), may hold values from -0.09375 to 0.09375
- b_down: float32 [1024], replicated, may hold values from -3 to 3
- ln1_gain: float32 [1024], replicated, may hold values from 0.5 to 1.5
- ln1_bias: float32 [1024], replicated, may hold values from -3 to 3
- ln2_gain: float32 [1024], replicated, may hold values from 0.5 to 1.5
- ln2_bias: float32 [1024], replicated, may hold values from -3 to 3
- kv_cache: bfloat16 [2, 16, 16384, 1024], P(None, None, 'req', 'tp'), may hold values from -122 to 122
- cache_len: int32 [16], replicated, may hold values from 0 to 16384, as said below
- span_len: int32 [16], replicated, may hold values from 1 to 512, as said below
Outputs:
- output: bfloat16 [8192, 1024], P(('req', 'tp'))
Inputs may be any that keep to these rules, and one draw needn't show every extreme that they name: The first cache_len[r] positions of request r hold its keys and values; some request has 16384. Slots from span_len[r] on are padding whose keys are not attended to; some request has 512.
All inputs are finite; a program needn't handle non-finite values.
Results may differ from a plain program's by a relative error of at most 0.015.
Values may be sent and summed in bfloat16 or wider, within the bound.
A program may use at most 256 MiB of HBM per device.

v0:
```python
import jax
import jax.numpy as jnp
from jax import lax
from jax.sharding import PartitionSpec as P

HEAD_DIM = 64
SPAN = 512
REQ_DEV = 1


masked_score = -1e30


def layer_norm(values, gain, bias):
    centre = jnp.mean(values, axis=-1, keepdims=True)
    centred = values - centre
    variance = jnp.mean(centred * centred, axis=-1, keepdims=True)
    return centred * lax.rsqrt(variance + 1e-05) * gain + bias


def partial_attention(queries, key_rows, value_rows, allowed):
    scores = jnp.einsum(
        "chd,nhd->hcn", queries, key_rows, preferred_element_type=jnp.float32
    ) * queries.shape[-1] ** (-0.5)
    scores = jnp.where(allowed[None], scores, masked_score)
    peaks = jnp.max(scores, axis=-1)
    weights = jnp.where(allowed[None], jnp.exp(scores - peaks[..., None]), 0.0).astype(jnp.bfloat16)
    weight_sums = jnp.sum(weights.astype(jnp.float32), axis=-1)
    blended = jnp.einsum("hcn,nhd->chd", weights, value_rows, preferred_element_type=jnp.float32)
    return (peaks.T, weight_sums.T, blended.reshape(blended.shape[0], -1))


def merge_axis(peaks, weight_sums, blended, axis):
    highest = jnp.max(peaks, axis=axis, keepdims=True)
    factors = jnp.exp(peaks - highest)
    sums_out = jnp.sum(factors * weight_sums, axis=axis)
    spread = jnp.repeat(factors, blended.shape[-1] // peaks.shape[-1], axis=-1)
    blend_out = jnp.sum(spread * blended, axis=axis)
    return (jnp.squeeze(highest, axis=axis), sums_out, blend_out)


def block_partials(queries, key_rows, value_rows, starts, lengths):
    total_blocks = key_rows.shape[0]
    block_width = key_rows.shape[1]
    group_size = 2

    def single(one_query, one_keys, one_values, start_pos, limit):
        places = start_pos + jnp.arange(block_width, dtype=jnp.int32)
        allowed = jnp.broadcast_to((places < limit)[None, :], (one_query.shape[0], block_width))
        return partial_attention(one_query, one_keys, one_values, allowed)

    def grouped(items):
        return jax.vmap(single)(*items)

    def regroup(member):
        return member.reshape((total_blocks // group_size, group_size) + member.shape[1:])

    results = lax.map(
        grouped,
        (
            regroup(queries),
            regroup(key_rows),
            regroup(value_rows),
            regroup(starts),
            regroup(lengths),
        ),
    )
    return tuple((member.reshape((total_blocks,) + member.shape[2:]) for member in results))


def shards(
    tokens,
    w_qkv,
    w_out,
    w_up,
    b_up,
    w_down,
    b_down,
    ln1_gain,
    ln1_bias,
    ln2_gain,
    ln2_bias,
    kv_cache,
    cache_len,
    span_len,
):
    width_here = w_qkv.shape[2]
    heads_here = width_here // HEAD_DIM
    block_len = kv_cache.shape[2]
    flat_qkv = w_qkv.reshape(w_qkv.shape[0], 3 * width_here)
    heads_qkv = jnp.dot(
        lax.all_gather(tokens, "tp", axis=0, tiled=True),
        flat_qkv,
        preferred_element_type=jnp.float32,
    ).astype(jnp.bfloat16)
    local_shape = (REQ_DEV, SPAN, heads_here, HEAD_DIM)
    queries = heads_qkv[:, :width_here].reshape(local_shape)
    fresh_keys = heads_qkv[:, width_here : 2 * width_here].reshape(local_shape)
    fresh_values = heads_qkv[:, 2 * width_here :].reshape(local_shape)
    where_req = lax.axis_index("req")
    own_span_len = lax.dynamic_slice_in_dim(span_len, where_req * REQ_DEV, REQ_DEV)
    positions = jnp.arange(SPAN, dtype=jnp.int32)

    def own_partial(one_query, one_keys, one_values, limit):
        allowed = (positions[None, :] <= positions[:, None]) & (positions[None, :] < limit)
        return partial_attention(one_query, one_keys, one_values, allowed)

    fresh = jax.vmap(own_partial)(queries, fresh_keys, fresh_values, own_span_len)
    every_query = lax.all_gather(heads_qkv[:, :width_here], "req", axis=0, tiled=True)
    every_query = every_query.reshape(-1, SPAN, heads_here, HEAD_DIM)
    request_total = every_query.shape[0]
    cached = kv_cache.reshape(2, request_total, block_len, heads_here, HEAD_DIM)
    starts = jnp.full((request_total,), where_req * block_len, jnp.int32)
    peaks, weight_sums, blended = block_partials(
        every_query, cached[0], cached[1], starts, cache_len
    )
    got_blended = lax.all_to_all(blended[:, None], "req", split_axis=0, concat_axis=1, tiled=True)
    got_peaks = lax.all_to_all(peaks[:, None], "req", split_axis=0, concat_axis=1, tiled=True)
    got_sums = lax.all_to_all(weight_sums[:, None], "req", split_axis=0, concat_axis=1, tiled=True)
    peaks, weight_sums, blended = merge_axis(got_peaks, got_sums, got_blended, 1)
    peaks, weight_sums, blended = merge_axis(
        jnp.stack([fresh[0], peaks]),
        jnp.stack([fresh[1], weight_sums]),
        jnp.stack([fresh[2], blended]),
        0,
    )
    attention = (
        (blended / jnp.repeat(weight_sums, HEAD_DIM, axis=-1))
        .astype(jnp.bfloat16)
        .reshape(-1, width_here)
    )
    projected = lax.psum_scatter(
        jnp.dot(attention, w_out, preferred_element_type=jnp.float32).astype(jnp.bfloat16),
        "tp",
        scatter_dimension=0,
        tiled=True,
    ).astype(jnp.float32)
    normed = layer_norm(tokens.astype(jnp.float32) + projected, ln1_gain, ln1_bias).astype(
        jnp.bfloat16
    )
    hidden = jax.nn.gelu(
        jnp.dot(
            lax.all_gather(normed, "tp", axis=0, tiled=True),
            w_up,
            preferred_element_type=jnp.float32,
        )
        + b_up,
        approximate=False,
    ).astype(jnp.bfloat16)
    summed = lax.psum_scatter(
        jnp.dot(hidden, w_down, preferred_element_type=jnp.float32).astype(jnp.bfloat16),
        "tp",
        scatter_dimension=0,
        tiled=True,
    ).astype(jnp.float32)
    return layer_norm(summed + b_down + normed.astype(jnp.float32), ln2_gain, ln2_bias).astype(
        jnp.bfloat16
    )


def solution(mesh):
    placed = (
        P(("req", "tp"), None),
        P(None, None, "tp"),
        P("tp", None),
        P(None, "tp"),
        P("tp"),
        P("tp", None),
        P(),
        P(),
        P(),
        P(),
        P(),
        P(None, None, "req", "tp"),
        P(),
        P(),
    )
    return jax.shard_map(
        shards, mesh=mesh, in_specs=placed, out_specs=P(("req", "tp"), None), check_vma=False
    )
```

profile of v0, /device:TPU:0, one launch (start us, length us, event | category | flops | bytes accessed | tf_op | source)
XLA Modules:
  0.0 1026.3 jit_solution(16349425846825280817)
XLA Ops:
  12.0 20.9 %all-gather.4.cloned.1.call-done = bf16[512,1024]{1,0:T(8,128)(2,1)} async-done(((bf16[256,1024]{1,0:T(8,128)(2,1)}), bf16[512,1024]{1,0:T(8,128)(2,1)}) %all-gather.4.cloned.1.call-update) | async-done | bytes 1048592 | tf_op jit(solution)/shard_map/all_gather | solution.py:92
  38.4 22.6 %fusion.68 = (bf16[1,16,1024,512]{3,2,1,0:T(8,128)(2,1)}, bf16[1,16,1024,512]{3,2,1,0:T(8,128)(2,1)}) fusion(bf16[2,16,1024,512]{3,2,1,0:T(8,128)(2,1)} %param.27), kind=kLoop, calls=%fused_computation.113 | loop fusion | bytes 67108864 | tf_op jit(solution)/shard_map/slice | solution.py:115
  61.0 22.0 %copy.36 = bf16[1,16,1024,512]{2,3,1,0:T(8,128)(2,1)} copy(bf16[1,16,1024,512]{3,2,1,0:T(8,128)(2,1)} %get-tuple-element.106) | data formatting | bytes 33554432 | tf_op jit(solution)/shard_map/slice | solution.py:115
  83.0 21.8 %copy.35 = bf16[1,16,1024,512]{2,3,1,0:T(8,128)(2,1)} copy(bf16[1,16,1024,512]{3,2,1,0:T(8,128)(2,1)} %get-tuple-element.107) | data formatting | bytes 33554432 | tf_op jit(solution)/shard_map/slice | solution.py:115
  113.3 21.2 %reshape.372 = bf16[8,2,512,8,64]{4,3,2,1,0:T(8,128)(2,1)} reshape(bf16[8192,512]{1,0:T(8,128)(2,1)} %all-gather.6.cloned.1.call-done) | data formatting | bytes 16777216 | tf_op jit(solution)/shard_map/reshape;reshape | solution.py:56
  134.5 18.3 %copy.37 = bf16[8,2,512,8,64]{2,4,3,1,0:T(8,128)(2,1)} copy(bf16[8,2,512,8,64]{4,3,2,1,0:T(8,128)(2,1)} %reshape.372) | data formatting | bytes 16777216 | tf_op jit(solution)/shard_map/while | solution.py:58
  152.8 371.9 %while.14 = (s32[]{:T(128)}, f32[8,2,512,8]{2,3,1,0:T(8,128)S(1)}, f32[8,2,512,8]{2,3,1,0:T(8,128)}, f32[8,2,512,512]{2,3,1,0:T(8,128)}, s32[8,2]{1,0:T(8,128)S(...) while((s32[]{:T(128)}, f32[8,2,512,8]{2,3,1,0:T(8,128)S(1)}, ...), condition=%wide.region_4.5_spmd, body=%wide.region_1.4_spmd.sunk | while | flops 2273300480 | bytes 112469160 | solution.py:58
  152.9 15.2 %fusion.88 = (f32[2,8,512]{2,1,0:T(8,128)S(1)}, f32[2,8,512,1024]{3,2,1,0:T(8,128)}) fusion(pred[2,1024]{1,0:T(4,128)(4,1)S(1)} %add_compare_fusion.2, bf16[8,2,1024,8,64]{2,4,3,1,0:T(8,128)(2,1)} %get-tuple-element.203, s32[]{:T(128)S(6)} %copy.50, bf16[8,2,512,8,64]{2,4,3,1,0:T(8,128)(2,1)} %get-tuple-element.202), kind=kOutput, calls=%fused_computation.3.clone.1 | convolution fusion | flops 1098899456 | bytes 36736000 | tf_op jit(solution)/shard_map/while/body/eval_jaxpr/vmap(chd,nhd->hcn)/dot_general | solution.py:22
  168.1 15.0 %convert_reduce_fusion.3 = f32[2,8,512]{2,1,0:T(8,128)S(1)} fusion(f32[2,8,512]{2,1,0:T(8,128)S(1)} %get-tuple-element.172, f32[2,8,512,1024]{3,2,1,0:T(8,128)} %get-tuple-element.173, pred[2,1024]{1,0:T(4,128)(4,1)S(1)} %add_compare_fusion.2), kind=kLoop, calls=%fused_computation.clone.1 | loop fusion | flops 58712064 | bytes 33622016 | tf_op jit(solution)/shard_map/while/body/eval_jaxpr/vmap()/reduce_sum | solution.py:28
  199.4 15.2 %fusion.88 = (f32[2,8,512]{2,1,0:T(8,128)S(1)}, f32[2,8,512,1024]{3,2,1,0:T(8,128)}) fusion(pred[2,1024]{1,0:T(4,128)(4,1)S(1)} %add_compare_fusion.2, bf16[8,2,1024,8,64]{2,4,3,1,0:T(8,128)(2,1)} %get-tuple-element.203, s32[]{:T(128)S(6)} %copy.50, bf16[8,2,512,8,64]{2,4,3,1,0:T(8,128)(2,1)} %get-tuple-element.202), kind=kOutput, calls=%fused_computation.3.clone.1 | convolution fusion | flops 1098899456 | bytes 36736000 | tf_op jit(solution)/shard_map/while/body/eval_jaxpr/vmap(chd,nhd->hcn)/dot_general | solution.py:22
  214.6 15.0 %convert_reduce_fusion.3 = f32[2,8,512]{2,1,0:T(8,128)S(1)} fusion(f32[2,8,512]{2,1,0:T(8,128)S(1)} %get-tuple-element.172, f32[2,8,512,1024]{3,2,1,0:T(8,128)} %get-tuple-element.173, pred[2,1024]{1,0:T(4,128)(4,1)S(1)} %add_compare_fusion.2), kind=kLoop, calls=%fused_computation.clone.1 | loop fusion | flops 58712064 | bytes 33622016 | tf_op jit(solution)/shard_map/while/body/eval_jaxpr/vmap()/reduce_sum | solution.py:28
  245.9 15.2 %fusion.88 = (f32[2,8,512]{2,1,0:T(8,128)S(1)}, f32[2,8,512,1024]{3,2,1,0:T(8,128)}) fusion(pred[2,1024]{1,0:T(4,128)(4,1)S(1)} %add_compare_fusion.2, bf16[8,2,1024,8,64]{2,4,3,1,0:T(8,128)(2,1)} %get-tuple-element.203, s32[]{:T(128)S(6)} %copy.50, bf16[8,2,512,8,64]{2,4,3,1,0:T(8,128)(2,1)} %get-tuple-element.202), kind=kOutput, calls=%fused_computation.3.clone.1 | convolution fusion | flops 1098899456 | bytes 36736000 | tf_op jit(solution)/shard_map/while/body/eval_jaxpr/vmap(chd,nhd->hcn)/dot_general | solution.py:22
  261.1 15.0 %convert_reduce_fusion.3 = f32[2,8,512]{2,1,0:T(8,128)S(1)} fusion(f32[2,8,512]{2,1,0:T(8,128)S(1)} %get-tuple-element.172, f32[2,8,512,1024]{3,2,1,0:T(8,128)} %get-tuple-element.173, pred[2,1024]{1,0:T(4,128)(4,1)S(1)} %add_compare_fusion.2), kind=kLoop, calls=%fused_computation.clone.1 | loop fusion | flops 58712064 | bytes 33622016 | tf_op jit(solution)/shard_map/while/body/eval_jaxpr/vmap()/reduce_sum | solution.py:28
  292.4 15.2 %fusion.88 = (f32[2,8,512]{2,1,0:T(8,128)S(1)}, f32[2,8,512,1024]{3,2,1,0:T(8,128)}) fusion(pred[2,1024]{1,0:T(4,128)(4,1)S(1)} %add_compare_fusion.2, bf16[8,2,1024,8,64]{2,4,3,1,0:T(8,128)(2,1)} %get-tuple-element.203, s32[]{:T(128)S(6)} %copy.50, bf16[8,2,512,8,64]{2,4,3,1,0:T(8,128)(2,1)} %get-tuple-element.202), kind=kOutput, calls=%fused_computation.3.clone.1 | convolution fusion | flops 1098899456 | bytes 36736000 | tf_op jit(solution)/shard_map/while/body/eval_jaxpr/vmap(chd,nhd->hcn)/dot_general | solution.py:22
  338.9 15.2 %fusion.88 = (f32[2,8,512]{2,1,0:T(8,128)S(1)}, f32[2,8,512,1024]{3,2,1,0:T(8,128)}) fusion(pred[2,1024]{1,0:T(4,128)(4,1)S(1)} %add_compare_fusion.2, bf16[8,2,1024,8,64]{2,4,3,1,0:T(8,128)(2,1)} %get-tuple-element.203, s32[]{:T(128)S(6)} %copy.50, bf16[8,2,512,8,64]{2,4,3,1,0:T(8,128)(2,1)} %get-tuple-element.202), kind=kOutput, calls=%fused_computation.3.clone.1 | convolution fusion | flops 1098899456 | bytes 36736000 | tf_op jit(solution)/shard_map/while/body/eval_jaxpr/vmap(chd,nhd->hcn)/dot_general | solution.py:22
  354.1 15.0 %convert_reduce_fusion.3 = f32[2,8,512]{2,1,0:T(8,128)S(1)} fusion(f32[2,8,512]{2,1,0:T(8,128)S(1)} %get-tuple-element.172, f32[2,8,512,1024]{3,2,1,0:T(8,128)} %get-tuple-element.173, pred[2,1024]{1,0:T(4,128)(4,1)S(1)} %add_compare_fusion.2), kind=kLoop, calls=%fused_computation.clone.1 | loop fusion | flops 58712064 | bytes 33622016 | tf_op jit(solution)/shard_map/while/body/eval_jaxpr/vmap()/reduce_sum | solution.py:28
  385.4 15.2 %fusion.88 = (f32[2,8,512]{2,1,0:T(8,128)S(1)}, f32[2,8,512,1024]{3,2,1,0:T(8,128)}) fusion(pred[2,1024]{1,0:T(4,128)(4,1)S(1)} %add_compare_fusion.2, bf16[8,2,1024,8,64]{2,4,3,1,0:T(8,128)(2,1)} %get-tuple-element.203, s32[]{:T(128)S(6)} %copy.50, bf16[8,2,512,8,64]{2,4,3,1,0:T(8,128)(2,1)} %get-tuple-element.202), kind=kOutput, calls=%fused_computation.3.clone.1 | convolution fusion | flops 1098899456 | bytes 36736000 | tf_op jit(solution)/shard_map/while/body/eval_jaxpr/vmap(chd,nhd->hcn)/dot_general | solution.py:22
  431.9 15.2 %fusion.88 = (f32[2,8,512]{2,1,0:T(8,128)S(1)}, f32[2,8,512,1024]{3,2,1,0:T(8,128)}) fusion(pred[2,1024]{1,0:T(4,128)(4,1)S(1)} %add_compare_fusion.2, bf16[8,2,1024,8,64]{2,4,3,1,0:T(8,128)(2,1)} %get-tuple-element.203, s32[]{:T(128)S(6)} %copy.50, bf16[8,2,512,8,64]{2,4,3,1,0:T(8,128)(2,1)} %get-tuple-element.202), kind=kOutput, calls=%fused_computation.3.clone.1 | convolution fusion | flops 1098899456 | bytes 36736000 | tf_op jit(solution)/shard_map/while/body/eval_jaxpr/vmap(chd,nhd->hcn)/dot_general | solution.py:22
  478.4 15.2 %fusion.88 = (f32[2,8,512]{2,1,0:T(8,128)S(1)}, f32[2,8,512,1024]{3,2,1,0:T(8,128)}) fusion(pred[2,1024]{1,0:T(4,128)(4,1)S(1)} %add_compare_fusion.2, bf16[8,2,1024,8,64]{2,4,3,1,0:T(8,128)(2,1)} %get-tuple-element.203, s32[]{:T(128)S(6)} %copy.50, bf16[8,2,512,8,64]{2,4,3,1,0:T(8,128)(2,1)} %get-tuple-element.202), kind=kOutput, calls=%fused_computation.3.clone.1 | convolution fusion | flops 1098899456 | bytes 36736000 | tf_op jit(solution)/shard_map/while/body/eval_jaxpr/vmap(chd,nhd->hcn)/dot_general | solution.py:22
  566.7 286.4 %all-to-all-done.1 = f32[16,1,512,512]{2,3,1,0:T(8,128)} async-done(((f32[16,1,512,512]{2,3,1,0:T(8,128)}), f32[16,1,512,512]{2,3,1,0:T(8,128)}, u32[]{:S(2)}, u32[]{:S(2)}) %all-to-all-start.1) | async-done | bytes 16777248 | tf_op jit(solution)/shard_map/all_to_all | solution.py:117
  865.5 85.8 %reduce-scatter.3.cloned.1.call-done = bf16[256,1024]{1,0:T(8,128)(2,1)} async-done(((bf16[512,1024]{1,0:T(8,128)(2,1)}), bf16[256,1024]{1,0:T(8,128)(2,1)}) %reduce-scatter.3.cloned.1.call-update) | async-done | bytes 524304 | tf_op jit(solution)/shard_map/reduce_scatter | solution.py:132
  956.4 21.2 %all-gather.8.cloned.1.call-done = bf16[512,1024]{1,0:T(8,128)(2,1)} async-done(((bf16[256,1024]{1,0:T(8,128)(2,1)}), bf16[512,1024]{1,0:T(8,128)(2,1)}) %all-gather.8.cloned.1.call-update) | async-done | bytes 1048592 | tf_op jit(solution)/shard_map/all_gather | solution.py:143
  977.6 16.8 %fusion.26 = bf16[512,1024]{1,0:T(8,128)(2,1)} fusion(bf16[2048,1024]{1,0:T(8,128)(2,1)} %param.21, bf16[512,1024]{1,0:T(8,128)(2,1)} %all-gather.8.cloned.1.call-done, bf16[1024,2048]{1,0:T(8,128)(2,1)} %param.19, f32[2048]{0:T(1024)S(1)} %copy-done.12), kind=kOutput, calls=%fused_computation.50 | convolution fusion | flops 4364697600 | bytes 10493952 | tf_op jit(solution)/shard_map/dot_general | solution.py:151
  994.5 20.5 %reduce-scatter.5.cloned.1.call-done = bf16[256,1024]{1,0:T(8,128)(2,1)} async-done(((bf16[512,1024]{1,0:T(8,128)(2,1)}), bf16[256,1024]{1,0:T(8,128)(2,1)}) %reduce-scatter.5.cloned.1.call-update) | async-done | bytes 524304 | tf_op jit(solution)/shard_map/reduce_scatter | solution.py:150
  (132 shorter events, 273.5 us)
Async XLA Ops:
  6.5 857.2 %copy-start = (bf16[512,1024]{1,0:T(8,128)(2,1)S(1)}, bf16[512,1024]{1,0:T(8,128)(2,1)}, u32[]{:S(2)}) copy-start(bf16[512,1024]{1,0:T(8,128)(2,1)} %param.18) | copy-start | bytes 3145732
  6.5 26.4 %all-gather.4.cloned.1.call-start = ((), (), s32[]{:S(2)}) async-start(), calls=%async_computation.5 | async-start | bytes 1572864 | tf_op jit(solution)/shard_map/all_gather | solution.py:92
  7.3 106.0 %all-gather.6.cloned.1.call-start = ((), (), s32[]{:S(2)}) async-start(), calls=%async_computation.6 | async-start | bytes 8912896 | tf_op jit(solution)/shard_map/all_gather | solution.py:109
  32.9 5.3 copy-start.11
  551.1 5.5 copy-start.13
  551.1 7.0 copy-start.3
  551.1 8.5 copy-start.4
  551.1 302.0 %all-to-all-start.1 = ((f32[16,1,512,512]{2,3,1,0:T(8,128)}), f32[16,1,512,512]{2,3,1,0:T(8,128)}, u32[]{:S(2)}, u32[]{:S(2)}) async-start(f32[16,1,512,512]{2,3,1,0:T(8,128)} %bitcast.105), calls=%async_computation.1 | async-start | bytes 33554432 | tf_op jit(solution)/shard_map/all_to_all | solution.py:117
  556.4 394.9 %reduce-scatter.3.cloned.1.call-start = ((), (), s32[]{:S(2)}) async-start(), calls=%async_computation.7 | async-start | bytes 1572864 | tf_op jit(solution)/shard_map/reduce_scatter | solution.py:132
  560.7 1.5 copy-start.5
  863.2 88.1 %copy-start.2 = (bf16[256,1024]{1,0:T(8,128)(2,1)S(1)}, bf16[256,1024]{1,0:T(8,128)(2,1)}, u32[]{:S(2)}) copy-start(bf16[256,1024]{1,0:T(8,128)(2,1)} %param.16) | copy-start | bytes 1572868
  863.5 90.4 %copy-start.7 = (f32[1024]{0:T(1024)S(1)}, f32[1024]{0:T(1024)}, u32[]{:S(2)}) copy-start(f32[1024]{0:T(1024)} %param.24) | copy-start | bytes 12292
  863.6 90.4 %copy-start.8 = (f32[1024]{0:T(1024)S(1)}, f32[1024]{0:T(1024)}, u32[]{:S(2)}) copy-start(f32[1024]{0:T(1024)} %param.23) | copy-start | bytes 12292
  863.7 113.9 %copy-start.12 = (f32[2048]{0:T(1024)S(1)}, f32[2048]{0:T(1024)}, u32[]{:S(2)}) copy-start(f32[2048]{0:T(1024)} %param.20) | copy-start | bytes 24580
  865.5 112.1 %all-gather.8.cloned.1.call-start = ((), (), s32[]{:S(2)}) async-start(), calls=%async_computation.8 | async-start | bytes 1572864 | tf_op jit(solution)/shard_map/all_gather | solution.py:143
  956.1 58.8 %copy-start.1 = (bf16[256,1024]{1,0:T(8,128)(2,1)S(1)}, bf16[256,1024]{1,0:T(8,128)(2,1)}, u32[]{:S(2)}) copy-start(bf16[256,1024]{1,0:T(8,128)(2,1)} %add_convert_fusion.1) | copy-start | bytes 1572868
  956.1 58.8 %copy-start.6 = (f32[1024]{0:T(1024)S(1)}, f32[1024]{0:T(1024)}, u32[]{:S(2)}) copy-start(f32[1024]{0:T(1024)} %param.22) | copy-start | bytes 12292
  956.1 61.5 %copy-start.9 = (f32[1024]{0:T(1024)S(1)}, f32[1024]{0:T(1024)}, u32[]{:S(2)}) copy-start(f32[1024]{0:T(1024)} %param.26) | copy-start | bytes 12292
  956.2 61.5 %copy-start.10 = (f32[1024]{0:T(1024)S(1)}, f32[1024]{0:T(1024)}, u32[]{:S(2)}) copy-start(f32[1024]{0:T(1024)} %param.25) | copy-start | bytes 12292
  956.2 58.8 %reduce-scatter.5.cloned.1.call-start = ((), (), s32[]{:S(2)}) async-start(), calls=%async_computation.9 | async-start | bytes 1572864 | tf_op jit(solution)/shard_map/reduce_scatter | solution.py:150
Sparse Core Ops, SparseCore 0:
  8.9 23.9 all-gather.3
  38.4 74.8 all-gather.5
  865.6 85.6 reduce-scatter.2
  956.2 21.3 all-gather.7
  994.6 20.3 reduce-scatter.4
where the time goes:
time: 1030 us
  waiting for transfers between devices  444 us (43%)
  matrix products  260 us (25%)
  other arithmetic  142 us (14%)
  local copies, waits for them, and re-layouts  134 us (13%)
  blocking collectives  26.4 us (3%)
  between operations  13.5 us (1%)
    all_to_all x1, waiting for transfers between devices, shards(): lax.all_to_all(blended[:, None], 'req', split_axis=0, concat_axis=1, tile...  286 us
    dot_general x9, matrix products, partial_attention(): jnp.einsum('chd,nhd->hcn', queries, key_rows, preferred_element_type=jnp....  123 us
    reduce_sum x9, other arithmetic, partial_attention(): weight_sums = jnp.sum(weights.astype(jnp.float32), axis=-1)  122 us
    dot_general x9, matrix products, partial_attention(): jnp.einsum('hcn,nhd->chd', weights, value_rows, preferred_element_type=jn...  115 us
    reduce_scatter x1, waiting for transfers between devices, shards(): lax.psum_scatter(jnp.dot(attention, w_out, preferred_element_type=jnp.flo...  85.8 us
    slice x2, local copies, waits for them, and re-layouts, shards(): cached[1]  44.6 us
    slice x1, local copies, waits for them, and re-layouts, shards(): cached[0]  21.8 us
    another operation x1, local copies, waits for them, and re-layouts, regroup(): member.reshape((total_blocks // group_size, group_size) + member.shape[1:])  21.2 us
  transfers between devices with their start and end apart: 6, of which 6 were waited for; matrix products, arithmetic and copies ran while one was open for 8% of the time, Pallas kernels for 0%

commit v1 on v0

v1 whole, which is shorter than its diff:
```python
import functools

import jax
import jax.numpy as jnp
from jax import lax
from jax.experimental import pallas as pl
from jax.experimental.pallas import tpu as pltpu
from jax.sharding import PartitionSpec as P

HEAD_DIM = 64
PAIR = 2 * HEAD_DIM
NEG = -1e30
ONES = 16
MESH = pl.DeviceIdType.MESH


def layer_norm(values, gain, bias):
    centre = jnp.mean(values, axis=-1, keepdims=True)
    centred = values - centre
    variance = jnp.mean(centred * centred, axis=-1, keepdims=True)
    return centred * lax.rsqrt(variance + 1e-05) * gain + bias


def ring_place(index, n):
    z, y, core = index // 4, (index // 2) % 2, index % 2
    chip = z + y * (n // 2 - 1 - 2 * z)
    return 2 * chip + core


def ring_index(place, n):
    chip, core = place // 2, place % 2
    y = chip // (n // 4)
    z = chip + y * (n // 2 - 1 - 2 * chip)
    return 4 * z + 2 * y + core


def attend(scores, v_t):
    peak = jnp.max(scores, axis=0, keepdims=True)
    weights = jnp.exp(scores - peak).astype(jnp.bfloat16)
    ones = jnp.ones((ONES, v_t.shape[1]), jnp.bfloat16)
    both = jnp.dot(
        jnp.concatenate([v_t, ones], axis=0), weights, preferred_element_type=jnp.float32
    )
    return peak, both[HEAD_DIM : HEAD_DIM + 1], both[:HEAD_DIM]


def ring_kernel(
    n,
    streams,
    len_ref,
    span_ref,
    q_ref,
    fk_ref,
    fv_ref,
    kv_ref,
    out_ref,
    q_buf,
    acc_buf,
    st_buf,
    kv_buf,
    bias_buf,
    loc_acc,
    loc_st,
    q_send,
    q_recv,
    a_send,
    a_recv,
    s_send,
    s_recv,
    kv_sem,
):
    width, slots = q_ref.shape
    keys = kv_buf.shape[3]
    lanes = width // streams
    heads = lanes // HEAD_DIM
    me = lax.axis_index("req")
    place = ring_place(me, n)
    right = ring_index((place + 1) % n, n)
    left = ring_index((place + n - 1) % n, n)
    onward = (right, left)

    barrier = pltpu.get_barrier_semaphore()
    for neighbour in (left, right):
        pl.semaphore_signal(barrier, inc=1, device_id={"req": neighbour}, device_id_type=MESH)

    def owner(j, s):
        return ring_index((place + n - s) % n if j == 0 else (place + s) % n, n)

    def rows(j):
        return pl.ds(j * lanes, lanes)

    def kv_copy(j, s):
        return pltpu.make_async_copy(
            kv_ref.at[:, owner(j, s), :, rows(j)], kv_buf.at[s % 2, j], kv_sem.at[s % 2, j]
        )

    def remote(src, dst, send, recv, j):
        return pltpu.make_async_remote_copy(
            src_ref=src,
            dst_ref=dst,
            send_sem=send,
            recv_sem=recv,
            device_id={"req": onward[j]},
            device_id_type=MESH,
        )

    def q_copy(j, s):
        return remote(
            q_buf.at[s, rows(j)], q_buf.at[s + 1, rows(j)], q_send.at[j, s], q_recv.at[j, s], j
        )

    def acc_copies(j, s):
        return (
            remote(
                acc_buf.at[s, rows(j)],
                acc_buf.at[s + 1, rows(j)],
                a_send.at[j, s],
                a_recv.at[j, s],
                j,
            ),
            remote(st_buf.at[s, j], st_buf.at[s + 1, j], s_send.at[j, s], s_recv.at[j, s], j),
        )

    for j in range(streams):
        kv_copy(j, 0).start()
    q_buf[0] = q_ref[...]
    pl.semaphore_wait(barrier, 2)

    lane = lax.broadcasted_iota(jnp.int32, (1, PAIR), 1)
    row = lax.broadcasted_iota(jnp.int32, (PAIR, 1), 0)
    keep = []
    spare = []
    for h in range(2):
        spare_at = HEAD_DIM * (1 - h)
        keep.append(jnp.where(lane == spare_at, 0.0, 1.0).astype(jnp.bfloat16))
        spare.append(spare_at)

    def masked_query(q_pair, h):
        own = q_pair[h * HEAD_DIM : (h + 1) * HEAD_DIM]
        first = lax.broadcasted_iota(jnp.int32, (HEAD_DIM, slots), 0) == 0
        other = jnp.where(first, 1.0, 0.0).astype(jnp.bfloat16)
        return jnp.concatenate([own, other] if h == 0 else [other, own], axis=0)

    def merged(j, slot, h):
        at = pl.ds(j * lanes + h * HEAD_DIM, HEAD_DIM)
        peak_a = st_buf[slot, j, h : h + 1, :]
        sum_a = st_buf[slot, j, heads + h : heads + h + 1, :]
        peak_b = loc_st[j, h : h + 1, :]
        sum_b = loc_st[j, heads + h : heads + h + 1, :]
        peak = jnp.maximum(peak_a, peak_b)
        fa = jnp.exp(peak_a - peak)
        fb = jnp.exp(peak_b - peak)
        blend = fa * acc_buf[slot, at, :].astype(jnp.float32) + fb * loc_acc[at, :]
        return at, peak, fa * sum_a + fb * sum_b, blend

    def step(s, carry):
        for j in range(streams):

            @pl.when(s + 1 < n)
            def _():
                kv_copy(j, s + 1).start()

            @pl.when(s > 0)
            def _():
                q_copy(j, s - 1).wait_recv()

            @pl.when(s + 1 < n)
            def _():
                q_copy(j, s).start()

        for j in range(streams):
            kv_copy(j, s).wait()
            limit = len_ref[owner(j, s)]
            position = me * keys + lax.broadcasted_iota(jnp.int32, (keys, PAIR), 0)
            lane_full = lax.broadcasted_iota(jnp.int32, (keys, PAIR), 1)
            for h in range(2):
                out = (position >= limit) & (lane_full == spare[h])
                bias_buf[h] = jnp.where(out, NEG, 0.0).astype(jnp.bfloat16)
            for g in range(lanes // PAIR):
                k_pair = kv_buf[s % 2, j, 0, :, g * PAIR : (g + 1) * PAIR]
                v_t = kv_buf[s % 2, j, 1, :, g * PAIR : (g + 1) * PAIR].T
                q_pair = q_buf[s, pl.ds(j * lanes + g * PAIR, PAIR), :]
                for h in range(2):
                    scores = jnp.dot(
                        k_pair * keep[h] + bias_buf[h],
                        masked_query(q_pair, h),
                        preferred_element_type=jnp.float32,
                    )
                    peak, total, blend = attend(scores, v_t[h * HEAD_DIM : (h + 1) * HEAD_DIM])
                    i = 2 * g + h
                    loc_st[j, i : i + 1, :] = peak
                    loc_st[j, heads + i : heads + i + 1, :] = total
                    loc_acc[pl.ds(j * lanes + i * HEAD_DIM, HEAD_DIM), :] = blend

            @pl.when(s == 0)
            def _():
                st_buf[0, j] = loc_st[j]
                acc_buf[0, rows(j), :] = loc_acc[rows(j), :].astype(jnp.bfloat16)

            @pl.when(s > 0)
            def _():
                for copy in acc_copies(j, s - 1):
                    copy.wait_recv()
                for h in range(heads):
                    at, peak, total, blend = merged(j, s, h)
                    st_buf[s, j, h : h + 1, :] = peak
                    st_buf[s, j, heads + h : heads + h + 1, :] = total
                    acc_buf[s, at, :] = blend.astype(jnp.bfloat16)

            for copy in acc_copies(j, s):
                copy.start()
        return carry

    lax.fori_loop(0, n, step, 0)

    limit = span_ref[me]
    key_at = lax.broadcasted_iota(jnp.int32, (slots, slots), 0)
    slot_at = lax.broadcasted_iota(jnp.int32, (slots, slots), 1)
    allowed = (key_at <= slot_at) & (key_at < limit)
    for j in range(streams):
        for g in range(lanes // PAIR):
            base = j * lanes + g * PAIR
            k_pair = fk_ref[:, base : base + PAIR]
            v_t = fv_ref[:, base : base + PAIR].T
            q_pair = q_ref[base : base + PAIR, :]
            for h in range(2):
                scores = jnp.dot(
                    k_pair * keep[h], masked_query(q_pair, h), preferred_element_type=jnp.float32
                )
                scores = jnp.where(allowed, scores, NEG)
                peak, total, blend = attend(scores, v_t[h * HEAD_DIM : (h + 1) * HEAD_DIM])
                i = 2 * g + h
                loc_st[j, i : i + 1, :] = peak
                loc_st[j, heads + i : heads + i + 1, :] = total
                loc_acc[pl.ds(j * lanes + i * HEAD_DIM, HEAD_DIM), :] = blend
    for j in range(streams):
        for copy in acc_copies(j, n - 1):
            copy.wait_recv()
        for h in range(heads):
            at, _, total, blend = merged(j, n, h)
            out_ref[at, :] = (blend / total).astype(jnp.bfloat16)

    def drain(s, carry):
        for j in range(streams):

            @pl.when(s + 1 < n)
            def _():
                q_copy(j, s).wait_send()

            for copy in acc_copies(j, s):
                copy.wait_send()
        return carry

    lax.fori_loop(0, n, drain, 0)


def ring_attention(n, q_t, fresh_k, fresh_v, kv, cache_len, span_len):
    width, slots = q_t.shape
    keys = kv.shape[2]
    streams = 2 if width % (2 * PAIR) == 0 else 1
    lanes = width // streams
    stat_rows = -(-2 * (lanes // HEAD_DIM) // 8) * 8
    requests = kv.shape[1]
    vmem = pl.BlockSpec(memory_space=pltpu.VMEM)
    smem = pl.BlockSpec(memory_space=pltpu.SMEM)
    dma = pltpu.SemaphoreType.DMA
    return pl.pallas_call(
        functools.partial(ring_kernel, n, streams),
        out_shape=jax.ShapeDtypeStruct((width, slots), jnp.bfloat16),
        in_specs=[smem, smem, vmem, vmem, vmem, pl.BlockSpec(memory_space=pl.ANY)],
        out_specs=vmem,
        scratch_shapes=[
            pltpu.VMEM((n, width, slots), jnp.bfloat16),
            pltpu.VMEM((n + 1, width, slots), jnp.bfloat16),
            pltpu.VMEM((n + 1, streams, stat_rows, slots), jnp.float32),
            pltpu.VMEM((2, streams, 2, keys, lanes), jnp.bfloat16),
            pltpu.VMEM((2, keys, PAIR), jnp.bfloat16),
            pltpu.VMEM((width, slots), jnp.float32),
            pltpu.VMEM((streams, stat_rows, slots), jnp.float32),
            dma((streams, n)),
            dma((streams, n)),
            dma((streams, n)),
            dma((streams, n)),
            dma((streams, n)),
            dma((streams, n)),
            dma((2, streams)),
        ],
        compiler_params=pltpu.CompilerParams(
            collective_id=0, has_side_effects=True, vmem_limit_bytes=56 * 1024 * 1024
        ),
        cost_estimate=pl.CostEstimate(
            flops=4 * requests * width * slots * keys,
            bytes_accessed=2 * requests * keys * width * 2,
            transcendentals=requests * (width // HEAD_DIM) * slots * keys,
        ),
    )(cache_len, span_len, q_t, fresh_k, fresh_v, kv)


def shards(
    n,
    tokens,
    w_qkv,
    w_out,
    w_up,
    b_up,
    w_down,
    b_down,
    ln1_gain,
    ln1_bias,
    ln2_gain,
    ln2_bias,
    kv_cache,
    cache_len,
    span_len,
):
    rows = lax.all_gather(tokens, "tp", axis=0, tiled=True)
    q_t = lax.dot_general(
        w_qkv[:, 0], rows, (((0,), (1,)), ((), ())), preferred_element_type=jnp.float32
    ).astype(jnp.bfloat16) * jnp.bfloat16(HEAD_DIM**-0.5)
    fresh_k = jnp.dot(rows, w_qkv[:, 1], preferred_element_type=jnp.float32).astype(jnp.bfloat16)
    fresh_v = jnp.dot(rows, w_qkv[:, 2], preferred_element_type=jnp.float32).astype(jnp.bfloat16)
    attention = ring_attention(n, q_t, fresh_k, fresh_v, kv_cache, cache_len, span_len)
    projected = lax.psum_scatter(
        lax.dot_general(
            attention, w_out, (((0,), (0,)), ((), ())), preferred_element_type=jnp.float32
        ).astype(jnp.bfloat16),
        "tp",
        scatter_dimension=0,
        tiled=True,
    ).astype(jnp.float32)
    normed = layer_norm(tokens.astype(jnp.float32) + projected, ln1_gain, ln1_bias).astype(
        jnp.bfloat16
    )
    hidden = jax.nn.gelu(
        jnp.dot(
            lax.all_gather(normed, "tp", axis=0, tiled=True),
            w_up,
            preferred_element_type=jnp.float32,
        )
        + b_up,
        approximate=False,
    ).astype(jnp.bfloat16)
    summed = lax.psum_scatter(
        jnp.dot(hidden, w_down, preferred_element_type=jnp.float32).astype(jnp.bfloat16),
        "tp",
        scatter_dimension=0,
        tiled=True,
    ).astype(jnp.float32)
    return layer_norm(summed + b_down + normed.astype(jnp.float32), ln2_gain, ln2_bias).astype(
        jnp.bfloat16
    )


def solution(mesh):
    placed = (
        P(("req", "tp"), None),
        P(None, None, "tp"),
        P("tp", None),
        P(None, "tp"),
        P("tp"),
        P("tp", None),
        P(),
        P(),
        P(),
        P(),
        P(),
        P(None, None, "req", "tp"),
        P(),
        P(),
    )
    return jax.shard_map(
        functools.partial(shards, mesh.shape["req"]),
        mesh=mesh,
        in_specs=placed,
        out_specs=P(("req", "tp"), None),
        check_vma=False,
    )
```

time: 1030 us -> 277 us (0.27)
  waiting for transfers between devices: 444 us -> 89.2 us
  matrix products: 260 us -> 28.6 us
  Pallas kernels: 0 us -> 135 us
  local copies, waits for them, and re-layouts: 134 us -> 0.06 us
  other arithmetic: 142 us -> 9.55 us
  blocking collectives: 26.4 us -> 0 us
    all_to_all x1 -> x0, waiting for transfers between devices: 286 us -> none  [shards(): lax.all_to_all(blended[:, None], 'req', split_axis=0, concat_axis=1, tile...]
    dot_general x20 -> x4, matrix products: 243 us -> 11.8 us  [the longest x1 3.14 us: shards(): jnp.dot(rows, w_qkv[:, 2], preferred_element_type=jnp.float32)]
    pallas_call x0 -> x1, Pallas kernels: none -> 135 us  [ring_attention(): pl.pallas_call(functools.partial(ring_kernel, n, streams), out_shape=jax....]
    reduce_sum x13 -> x0, other arithmetic: 130 us -> none  [the longest x9 122 us: partial_attention(): weight_sums = jnp.sum(weights.astype(jnp.float32), axis=-1)]
    slice x7 -> x0, local copies, waits for them, and re-layouts: 70.1 us -> none  [the longest x2 44.6 us: shards(): cached[1]]
    reduce_scatter x1, waiting for transfers between devices: 85.8 us -> 21.2 us  [shards(): lax.psum_scatter(lax.dot_general(attention, w_out, (((0,), (0,)), ((), ()...]
    all_to_all x2 -> x0, blocking collectives: 26.4 us -> none  [the longest x1 13.5 us: shards(): lax.all_to_all(weight_sums[:, None], 'req', split_axis=0, concat_axis=1,...]
    another operation x1 -> x0, local copies, waits for them, and re-layouts: 21.2 us -> none  [regroup(): member.reshape((total_blocks // group_size, group_size) + member.shape[1:])]
  transfers between devices with their start and end apart: 6 -> 4, of which waited for: 6 -> 4; matrix products, arithmetic and copies ran while one was open for 8% -> 0% of each run, Pallas kernels for 0% -> 0%
where the time goes in v1:
time: 277 us; the launch traced here: 276 us
  Pallas kernels  135 us (49%)
  waiting for transfers between devices  89.2 us (32%)
  matrix products  28.6 us (10%)
  between operations  13.2 us (5%)
  other arithmetic  9.55 us (3%)
    pallas_call x1, Pallas kernels, ring_attention(): pl.pallas_call(functools.partial(ring_kernel, n, streams), out_shape=jax....  135 us
    all_gather x1, waiting for transfers between devices, shards(): rows = lax.all_gather(tokens, 'tp', axis=0, tiled=True)  25.6 us
    all_gather x1, waiting for transfers between devices, shards(): lax.all_gather(normed, 'tp', axis=0, tiled=True)  21.2 us
    reduce_scatter x1, waiting for transfers between devices, shards(): lax.psum_scatter(lax.dot_general(attention, w_out, (((0,), (0,)), ((), ()...  21.2 us
    reduce_scatter x1, waiting for transfers between devices, shards(): lax.psum_scatter(jnp.dot(hidden, w_down, preferred_element_type=jnp.float...  20.5 us
    dot_general x1, matrix products, shards(): jnp.dot(hidden, w_down, preferred_element_type=jnp.float32)  16.8 us
  transfers between devices with their start and end apart: 4, of which 4 were waited for; matrix products, arithmetic and copies ran while one was open for 0% of the time, Pallas kernels for 0%

profile of v1, /device:TPU:0, one launch (start us, length us, event | category | flops | bytes accessed | tf_op | source)
XLA Modules:
  0.0 276.4 jit_solution(6089838230402079397)
XLA Ops:
  6.5 0.7 all-gather.3.cloned.1.call-update
  7.3 0.0 reduce-scatter.3.cloned.1.call-start
  7.3 25.6 %all-gather.3.cloned.1.call-done = bf16[512,1024]{1,0:T(8,128)(2,1)} async-done(((bf16[256,1024]{1,0:T(8,128)(2,1)}), bf16[512,1024]{1,0:T(8,128)(2,1)}) %all-gather.3.cloned.1.call-update) | async-done | bytes 1048592 | tf_op jit(solution)/shard_map/all_gather | solution.py:316
  32.9 3.1 %convolution_convert_fusion.1.fv_ref = bf16[512,512]{1,0:T(8,128)(2,1)} fusion(bf16[512,1024]{1,0:T(8,128)(2,1)} %all-gather.3.cloned.1.call-done, bf16[1024,3,512]{2,0,1:T(8,128)(2,1)} %param.15), kind=kOutput, calls=%fused_computation.22 | convolution fusion | flops 537133056 | bytes 2621440 | tf_op jit(solution)/shard_map/dot_general | solution.py:321
  36.1 3.0 %convolution_convert_fusion.2.fk_ref = bf16[512,512]{1,0:T(8,128)(2,1)} fusion(bf16[512,1024]{1,0:T(8,128)(2,1)} %all-gather.3.cloned.1.call-done, bf16[1024,3,512]{2,0,1:T(8,128)(2,1)} %param.15), kind=kOutput, calls=%fused_computation.23 | convolution fusion | flops 537133056 | bytes 2621440 | tf_op jit(solution)/shard_map/dot_general | solution.py:320
  39.1 2.8 %fusion.12.q_ref = bf16[512,512]{1,0:T(8,128)(2,1)} fusion(bf16[512,1024]{1,0:T(8,128)(2,1)S(1)} %copy-done.8, bf16[1024,3,512]{2,0,1:T(8,128)(2,1)} %param.15), kind=kOutput, calls=%fused_computation.25 | convolution fusion | flops 537395200 | bytes 2621440 | tf_op jit(solution)/shard_map/dot_general | solution.py:317
  41.9 135.5 %shard_map.136 = bf16[512,512]{1,0:T(8,128)(2,1)} custom-call(s32[16]{0:T(128)} %len_ref.1, s32[16]{0:T(128)} %span_ref.1, bf16[512,512]{1,0:T(8,128)(2,1)} %fusion.12.q_ref, bf16[512,512]{1,0:T(8,128)(2,1)} %convolution_convert_fusion.2.fk_ref, bf16[512,512]{1,0:T(8,128)(2,1)} %convolution_convert_fusion.1.fv_ref, bf16[2,16,1024,512]{3,2,1,0:T(8,128)(2,1)} %kv_ref.1), custom_call_target="tpu_custom_call" | custom-call | flops 17179869184 | bytes 33554432 | tf_op jit(solution)/shard_map/pallas_call | solution.py:267
  177.4 0.0 copy-start.4
  177.4 2.8 %convolution_convert_fusion = bf16[512,1024]{1,0:T(8,128)(2,1)} fusion(bf16[512,512]{1,0:T(8,128)(2,1)} %shard_map.136, bf16[512,1024]{1,0:T(8,128)(2,1)S(1)} %copy-done), kind=kOutput, calls=%fused_computation.21 | convolution fusion | flops 537395200 | bytes 2621440 | tf_op jit(solution)/shard_map/dot_general | solution.py:324
  180.2 0.0 reduce-scatter.3.cloned.1.call-update
  180.3 0.0 all-gather.5.cloned.1.call-start
  180.3 21.2 %reduce-scatter.3.cloned.1.call-done = bf16[256,1024]{1,0:T(8,128)(2,1)} async-done(((bf16[512,1024]{1,0:T(8,128)(2,1)}), bf16[256,1024]{1,0:T(8,128)(2,1)}) %reduce-scatter.3.cloned.1.call-update) | async-done | bytes 524304 | tf_op jit(solution)/shard_map/reduce_scatter | solution.py:323
  201.5 1.3 fusion.20
  202.8 1.3 multiply_reduce_fusion.1
  204.1 2.1 add_convert_fusion.1
  206.2 0.0 all-gather.5.cloned.1.call-update
  206.3 0.2 reduce-scatter.5.cloned.1.call-start
  206.5 21.2 %all-gather.5.cloned.1.call-done = bf16[512,1024]{1,0:T(8,128)(2,1)} async-done(((bf16[256,1024]{1,0:T(8,128)(2,1)}), bf16[512,1024]{1,0:T(8,128)(2,1)}) %all-gather.5.cloned.1.call-update) | async-done | bytes 1048592 | tf_op jit(solution)/shard_map/all_gather | solution.py:336
  227.8 16.8 %fusion.11 = bf16[512,1024]{1,0:T(8,128)(2,1)} fusion(bf16[2048,1024]{1,0:T(8,128)(2,1)} %param.19, bf16[512,1024]{1,0:T(8,128)(2,1)} %all-gather.5.cloned.1.call-done, bf16[1024,2048]{1,0:T(8,128)(2,1)} %param.17, f32[2048]{0:T(1024)S(1)} %copy-done.9), kind=kOutput, calls=%fused_computation.20 | convolution fusion | flops 4364697600 | bytes 10493952 | tf_op jit(solution)/shard_map/dot_general | solution.py:344
  244.6 0.0 reduce-scatter.5.cloned.1.call-update
  244.6 20.5 %reduce-scatter.5.cloned.1.call-done = bf16[256,1024]{1,0:T(8,128)(2,1)} async-done(((bf16[512,1024]{1,0:T(8,128)(2,1)}), bf16[256,1024]{1,0:T(8,128)(2,1)}) %reduce-scatter.5.cloned.1.call-update) | async-done | bytes 524304 | tf_op jit(solution)/shard_map/reduce_scatter | solution.py:343
  265.1 1.3 fusion.21
  266.4 1.4 multiply_reduce_fusion
  267.8 2.1 add_convert_fusion
  (24 shorter events, 0.1 us)
Async XLA Ops:
  6.5 170.9 %copy-start = (bf16[512,1024]{1,0:T(8,128)(2,1)S(1)}, bf16[512,1024]{1,0:T(8,128)(2,1)}, u32[]{:S(2)}) copy-start(bf16[512,1024]{1,0:T(8,128)(2,1)} %param.16) | copy-start | bytes 3145732
  6.5 26.4 %all-gather.3.cloned.1.call-start = ((), (), s32[]{:S(2)}) async-start(), calls=%async_computation.2 | async-start | bytes 1572864 | tf_op jit(solution)/shard_map/all_gather | solution.py:316
  7.3 194.2 %reduce-scatter.3.cloned.1.call-start = ((), (), s32[]{:S(2)}) async-start(), calls=%async_computation.3 | async-start | bytes 1572864 | tf_op jit(solution)/shard_map/reduce_scatter | solution.py:323
  32.9 6.2 %copy-start.8 = (bf16[512,1024]{1,0:T(8,128)(2,1)S(1)}, bf16[512,1024]{1,0:T(8,128)(2,1)}, u32[]{:S(2)}) copy-start(bf16[512,1024]{1,0:T(8,128)(2,1)} %all-gather.3.cloned.1.call-done) | copy-start | bytes 3145732
  177.4 24.1 %copy-start.2 = (bf16[256,1024]{1,0:T(8,128)(2,1)S(1)}, bf16[256,1024]{1,0:T(8,128)(2,1)}, u32[]{:S(2)}) copy-start(bf16[256,1024]{1,0:T(8,128)(2,1)} %param.14) | copy-start | bytes 1572868
  177.4 26.7 %copy-start.4 = (f32[1024]{0:T(1024)S(1)}, f32[1024]{0:T(1024)}, u32[]{:S(2)}) copy-start(f32[1024]{0:T(1024)} %param.22) | copy-start | bytes 12292
  177.4 26.7 %copy-start.5 = (f32[1024]{0:T(1024)S(1)}, f32[1024]{0:T(1024)}, u32[]{:S(2)}) copy-start(f32[1024]{0:T(1024)} %param.21) | copy-start | bytes 12292
  177.4 50.3 %copy-start.9 = (f32[2048]{0:T(1024)S(1)}, f32[2048]{0:T(1024)}, u32[]{:S(2)}) copy-start(f32[2048]{0:T(1024)} %param.18) | copy-start | bytes 24580
  180.3 47.5 %all-gather.5.cloned.1.call-start = ((), (), s32[]{:S(2)}) async-start(), calls=%async_computation.4 | async-start | bytes 1572864 | tf_op jit(solution)/shard_map/all_gather | solution.py:336
  206.3 58.8 %copy-start.1 = (bf16[256,1024]{1,0:T(8,128)(2,1)S(1)}, bf16[256,1024]{1,0:T(8,128)(2,1)}, u32[]{:S(2)}) copy-start(bf16[256,1024]{1,0:T(8,128)(2,1)} %add_convert_fusion.1) | copy-start | bytes 1572868
  206.3 58.8 %copy-start.3 = (f32[1024]{0:T(1024)S(1)}, f32[1024]{0:T(1024)}, u32[]{:S(2)}) copy-start(f32[1024]{0:T(1024)} %param.20) | copy-start | bytes 12292
  206.3 61.5 %copy-start.6 = (f32[1024]{0:T(1024)S(1)}, f32[1024]{0:T(1024)}, u32[]{:S(2)}) copy-start(f32[1024]{0:T(1024)} %param.24) | copy-start | bytes 12292
  206.3 61.5 %copy-start.7 = (f32[1024]{0:T(1024)S(1)}, f32[1024]{0:T(1024)}, u32[]{:S(2)}) copy-start(f32[1024]{0:T(1024)} %param.23) | copy-start | bytes 12292
  206.3 58.7 %reduce-scatter.5.cloned.1.call-start = ((), (), s32[]{:S(2)}) async-start(), calls=%async_computation.5 | async-start | bytes 1572864 | tf_op jit(solution)/shard_map/reduce_scatter | solution.py:343
Sparse Core Ops, SparseCore 0:
  8.9 23.9 all-gather.2
  180.4 21.0 reduce-scatter.2
  206.4 21.3 all-gather.4
  244.7 20.3 reduce-scatter.4

commit v2 on v1

--- a/solution.py
+++ b/solution.py
@@ -36,7 +36,7 @@
 
 def attend(scores, v_t):
     peak = jnp.max(scores, axis=0, keepdims=True)
-    weights = jnp.exp(scores - peak).astype(jnp.bfloat16)
+    weights = jnp.exp((scores - peak).astype(jnp.bfloat16))
     ones = jnp.ones((ONES, v_t.shape[1]), jnp.bfloat16)
     both = jnp.dot(
         jnp.concatenate([v_t, ones], axis=0), weights, preferred_element_type=jnp.float32
@@ -176,21 +176,29 @@
             for h in range(2):
                 out = (position >= limit) & (lane_full == spare[h])
                 bias_buf[h] = jnp.where(out, NEG, 0.0).astype(jnp.bfloat16)
-            for g in range(lanes // PAIR):
+            def scores_of(i):
+                g, h = i // 2, i % 2
                 k_pair = kv_buf[s % 2, j, 0, :, g * PAIR : (g + 1) * PAIR]
-                v_t = kv_buf[s % 2, j, 1, :, g * PAIR : (g + 1) * PAIR].T
                 q_pair = q_buf[s, pl.ds(j * lanes + g * PAIR, PAIR), :]
-                for h in range(2):
-                    scores = jnp.dot(
-                        k_pair * keep[h] + bias_buf[h],
-                        masked_query(q_pair, h),
-                        preferred_element_type=jnp.float32,
-                    )
-                    peak, total, blend = attend(scores, v_t[h * HEAD_DIM : (h + 1) * HEAD_DIM])
-                    i = 2 * g + h
-                    loc_st[j, i : i + 1, :] = peak
-                    loc_st[j, heads + i : heads + i + 1, :] = total
-                    loc_acc[pl.ds(j * lanes + i * HEAD_DIM, HEAD_DIM), :] = blend
+                return jnp.dot(
+                    k_pair * keep[h] + bias_buf[h],
+                    masked_query(q_pair, h),
+                    preferred_element_type=jnp.float32,
+                )
+
+            later = scores_of(0)
+            v_t = None
+            for i in range(heads):
+                scores = later
+                if i + 1 < heads:
+                    later = scores_of(i + 1)
+                g, h = i // 2, i % 2
+                if h == 0:
+                    v_t = kv_buf[s % 2, j, 1, :, g * PAIR : (g + 1) * PAIR].T
+                peak, total, blend = attend(scores, v_t[h * HEAD_DIM : (h + 1) * HEAD_DIM])
+                loc_st[j, i : i + 1, :] = peak
+                loc_st[j, heads + i : heads + i + 1, :] = total
+                loc_acc[pl.ds(j * lanes + i * HEAD_DIM, HEAD_DIM), :] = blend
 
             @pl.when(s == 0)
             def _():
@@ -298,6 +306,7 @@
 
 def shards(
     n,
+    tp,
     tokens,
     w_qkv,
     w_out,
@@ -313,39 +322,64 @@
     cache_len,
     span_len,
 ):
-    rows = lax.all_gather(tokens, "tp", axis=0, tiled=True)
-    q_t = lax.dot_general(
-        w_qkv[:, 0], rows, (((0,), (1,)), ((), ())), preferred_element_type=jnp.float32
-    ).astype(jnp.bfloat16) * jnp.bfloat16(HEAD_DIM**-0.5)
-    fresh_k = jnp.dot(rows, w_qkv[:, 1], preferred_element_type=jnp.float32).astype(jnp.bfloat16)
-    fresh_v = jnp.dot(rows, w_qkv[:, 2], preferred_element_type=jnp.float32).astype(jnp.bfloat16)
-    attention = ring_attention(n, q_t, fresh_k, fresh_v, kv_cache, cache_len, span_len)
-    projected = lax.psum_scatter(
-        lax.dot_general(
-            attention, w_out, (((0,), (0,)), ((), ())), preferred_element_type=jnp.float32
-        ).astype(jnp.bfloat16),
-        "tp",
-        scatter_dimension=0,
-        tiled=True,
-    ).astype(jnp.float32)
-    normed = layer_norm(tokens.astype(jnp.float32) + projected, ln1_gain, ln1_bias).astype(
-        jnp.bfloat16
+    index = lax.axis_index("tp")
+    half = tokens.shape[0]
+
+    def f32_dot(a, b, dims):
+        return lax.dot_general(a, b, (dims, ((), ())), preferred_element_type=jnp.float32)
+
+    def ordered(own, other, axis):
+        return jnp.where(
+            index == 0,
+            jnp.concatenate([own, other], axis=axis),
+            jnp.concatenate([other, own], axis=axis),
+        )
+
+    def queries(rows):
+        return f32_dot(w_qkv[:, 0], rows, ((0,), (1,))).astype(jnp.bfloat16) * jnp.bfloat16(
+            HEAD_DIM**-0.5
+        )
+
+    def fresh(rows, which):
+        return f32_dot(rows, w_qkv[:, which], ((1,), (0,))).astype(jnp.bfloat16)
+
+    def feed_forward(rows):
+        hidden = jax.nn.gelu(f32_dot(rows, w_up, ((1,), (0,))) + b_up, approximate=False)
+        return f32_dot(hidden.astype(jnp.bfloat16), w_down, ((1,), (0,)))
+
+    def first_norm(projected):
+        return layer_norm(tokens.astype(jnp.float32) + projected, ln1_gain, ln1_bias).astype(
+            jnp.bfloat16
+        )
+
+    if tp == 2:
+        swap = functools.partial(lax.ppermute, axis_name="tp", perm=[(0, 1), (1, 0)])
+        rows = ordered(tokens, swap(tokens), 0)
+    else:
+        rows = lax.all_gather(tokens, "tp", axis=0, tiled=True)
+    attention = ring_attention(
+        n, queries(rows), fresh(rows, 1), fresh(rows, 2), kv_cache, cache_len, span_len
     )
-    hidden = jax.nn.gelu(
-        jnp.dot(
-            lax.all_gather(normed, "tp", axis=0, tiled=True),
-            w_up,
-            preferred_element_type=jnp.float32,
-        )
-        + b_up,
-        approximate=False,
-    ).astype(jnp.bfloat16)
-    summed = lax.psum_scatter(
-        jnp.dot(hidden, w_down, preferred_element_type=jnp.float32).astype(jnp.bfloat16),
-        "tp",
-        scatter_dimension=0,
-        tiled=True,
-    ).astype(jnp.float32)
+    if tp == 2:
+        mine = lax.dynamic_slice_in_dim(attention, index * half, half, 1)
+        theirs = lax.dynamic_slice_in_dim(attention, (1 - index) * half, half, 1)
+        got = swap(f32_dot(theirs, w_out, ((0,), (0,))).astype(jnp.bfloat16))
+        normed = first_norm(f32_dot(mine, w_out, ((0,), (0,))) + got.astype(jnp.float32))
+        their_rows, summed = lax.optimization_barrier((swap(normed), feed_forward(normed)))
+        part = half // 2
+        back = [
+            swap(feed_forward(their_rows[i * part : (i + 1) * part]).astype(jnp.bfloat16))
+            for i in range(2)
+        ]
+        summed = summed + jnp.concatenate(back, axis=0).astype(jnp.float32)
+    else:
+        scatter = functools.partial(
+            lax.psum_scatter, axis_name="tp", scatter_dimension=0, tiled=True
+        )
+        projected = scatter(f32_dot(attention, w_out, ((0,), (0,))).astype(jnp.bfloat16))
+        normed = first_norm(projected.astype(jnp.float32))
+        all_rows = lax.all_gather(normed, "tp", axis=0, tiled=True)
+        summed = scatter(feed_forward(all_rows).astype(jnp.bfloat16)).astype(jnp.float32)
     return layer_norm(summed + b_down + normed.astype(jnp.float32), ln2_gain, ln2_bias).astype(
         jnp.bfloat16
     )
@@ -369,7 +403,7 @@
         P(),
     )
     return jax.shard_map(
-        functools.partial(shards, mesh.shape["req"]),
+        functools.partial(shards, mesh.shape["req"], mesh.shape["tp"]),
         mesh=mesh,
         in_specs=placed,
         out_specs=P(("req", "tp"), None),

time: 277 us -> 201 us (0.73)
  waiting for transfers between devices: 89.2 us -> 38.3 us
  Pallas kernels: 135 us -> 115 us
  between operations: 13.2 us -> 0.13 us
  starting transfers between devices: 0.31 us -> 9.08 us
  other arithmetic: 9.55 us -> 3.09 us
  matrix products: 28.6 us -> 34.7 us
    all_gather x2 -> x0, waiting for transfers between devices: 46.8 us -> none  [the longest x1 25.6 us: shards(): rows = lax.all_gather(tokens, 'tp', axis=0, tiled=True)]
    reduce_scatter x2 -> x0, waiting for transfers between devices: 41.6 us -> none  [the longest x1 21.2 us: shards(): lax.psum_scatter(lax.dot_general(attention, w_out, (((0,), (0,)), ((), ()...]
    ppermute x0 -> x5, waiting for transfers between devices: none -> 38.3 us  [the longest x2 12.3 us: shards(): swap(feed_forward(their_rows[i * part:(i + 1) * part]).astype(jnp.bfloat16))]
    pallas_call x1, Pallas kernels: 135 us -> 115 us  [ring_attention(): pl.pallas_call(functools.partial(ring_kernel, n, streams), out_shape=jax....]
    ppermute x0 -> x5, starting transfers between devices: none -> 9.08 us  [the longest x1 2.94 us: shards(): rows = ordered(tokens, swap(tokens), 0)]
    dot_general x5 -> x8, matrix products: 28.6 us -> 34.7 us  [f32_dot(): lax.dot_general(a, b, (dims, ((), ())), preferred_element_type=jnp.float32)]
  transfers between devices with their start and end apart: 4 -> 5, of which waited for: 4 -> 5; matrix products, arithmetic and copies ran while one was open for 0% -> 5% of each run, Pallas kernels for 0% -> 0%
where the time goes in v2:
time: 201 us; the launch traced here: 200 us
  Pallas kernels  115 us (57%)
  waiting for transfers between devices  38.3 us (19%)
  matrix products  34.7 us (17%)
  starting transfers between devices  9.08 us (5%)
  other arithmetic  3.09 us (2%)
    pallas_call x1, Pallas kernels, ring_attention(): pl.pallas_call(functools.partial(ring_kernel, n, streams), out_shape=jax....  115 us
    dot_general x8, matrix products, f32_dot(): lax.dot_general(a, b, (dims, ((), ())), preferred_element_type=jnp.float32)  34.7 us
    ppermute x2, waiting for transfers between devices, shards(): swap(feed_forward(their_rows[i * part:(i + 1) * part]).astype(jnp.bfloat16))  12.3 us
    ppermute x1, waiting for transfers between devices, shards(): rows = ordered(tokens, swap(tokens), 0)  12.1 us
    ppermute x1, waiting for transfers between devices, shards(): got = swap(f32_dot(theirs, w_out, ((0,), (0,))).astype(jnp.bfloat16))  11.4 us
  transfers between devices with their start and end apart: 5, of which 5 were waited for; matrix products, arithmetic and copies ran while one was open for 5% of the time, Pallas kernels for 0%

profile of v2, /device:TPU:0, one launch (start us, length us, event | category | flops | bytes accessed | tf_op | source)
XLA Modules:
  0.0 200.3 jit_solution(11893713896408898390)
XLA Ops:
  0.0 2.9 %collective-permute-start = (bf16[256,1024]{1,0:T(8,128)(2,1)}, bf16[256,1024]{1,0:T(8,128)(2,1)S(1)}, u32[]{:S(2)}, u32[]{:S(2)}) collective-permute-start(bf16[256,1024]{1,0:T(8,128)(2,1)} %param.14), channel_id=1, source_target_pairs={{0,1},{1,0},{2,3},{3,2},{4,5},{5,4},{6,7},{7,6},{8,9},{9,8},{10,11... | collective-permute-start | bytes 1572872 | tf_op jit(solution)/shard_map/ppermute | solution.py:357
  2.9 12.1 %collective-permute-done = bf16[256,1024]{1,0:T(8,128)(2,1)S(1)} collective-permute-done((bf16[256,1024]{1,0:T(8,128)(2,1)}, bf16[256,1024]{1,0:T(8,128)(2,1)S(1)}, u32[]{:S(2)}, u32[]{:S(2)}) %collective-permute-start) | collective-permute-done | bytes 524320 | tf_op jit(solution)/shard_map/ppermute | solution.py:357
  15.1 3.1 %convolution_convert_fusion.2.fk_ref = bf16[512,512]{1,0:T(8,128)(2,1)} fusion(bf16[1024,3,512]{2,0,1:T(8,128)(2,1)} %param.15, bf16[256,1024]{1,0:T(8,128)(2,1)S(1)} %collective-permute-done, bf16[256,1024]{1,0:T(8,128)(2,1)} %param.14, pred[]{:T(512)S(6)} %eq.3), kind=kOutput, calls=%fused_computation.26 | convolution fusion | flops 541851648 | bytes 2621441 | tf_op jit(solution)/shard_map/dot_general | solution.py:329
  18.2 1.5 convolution_convert_fusion.1.fv_ref
  19.7 1.6 fusion.11.q_ref
  21.3 115.0 %shard_map.136 = bf16[512,512]{1,0:T(8,128)(2,1)} custom-call(s32[16]{0:T(128)} %len_ref.1, s32[16]{0:T(128)} %span_ref.1, bf16[512,512]{1,0:T(8,128)(2,1)} %fusion.11.q_ref, bf16[512,512]{1,0:T(8,128)(2,1)} %convolution_convert_fusion.2.fk_ref, bf16[512,512]{1,0:T(8,128)(2,1)} %convolution_convert_fusion.1.fv_ref, bf16[2,16,1024,512]{3,2,1,0:T(8,128)(2,1)} %kv_ref.1), custom_call_target="tpu_custom_call" | custom-call | flops 17179869184 | bytes 33554432 | tf_op jit(solution)/shard_map/pallas_call | solution.py:275
  136.3 1.4 convolution_convert_fusion
  137.7 1.8 collective-permute-start.1
  139.5 11.4 %collective-permute-done.1 = bf16[256,1024]{1,0:T(8,128)(2,1)S(1)} collective-permute-done((bf16[256,1024]{1,0:T(8,128)(2,1)S(1)}, bf16[256,1024]{1,0:T(8,128)(2,1)S(1)}, u32[]{:S(2)}, u32[]{:S(2)}) %collective-permute-start.1) | collective-permute-done | bytes 524320 | tf_op jit(solution)/shard_map/ppermute | solution.py:366
  150.9 1.5 fusion.235
  152.5 0.2 multiply_reduce_fusion.1
  152.8 1.0 add_convert_fusion.1
  153.8 2.0 %collective-permute-start.2 = (bf16[256,1024]{1,0:T(8,128)(2,1)}, bf16[256,1024]{1,0:T(8,128)(2,1)}, u32[]{:S(2)}, u32[]{:S(2)}) collective-permute-start(bf16[256,1024]{1,0:T(8,128)(2,1)} %add_convert_fusion.1), channel_id=1, source_target_pairs={{0,1},{1,0},{2,3},{3,2},{4,5},{5,4},{6,7},{7,6},{8,9},{9,8},{10,11... | collective-permute-start | bytes 1572872 | tf_op jit(solution)/shard_map/ppermute | solution.py:368
  155.9 10.3 %fusion.12 = f32[256,1024]{1,0:T(8,128)S(1)} fusion(bf16[2048,1024]{1,0:T(8,128)(2,1)} %param.19, bf16[256,1024]{1,0:T(8,128)(2,1)} %add_convert_fusion.1, bf16[1024,2048]{1,0:T(8,128)(2,1)} %param.17, f32[2048]{0:T(1024)S(1)} %copy-done.8), kind=kOutput, calls=%fused_computation.32 | convolution fusion | flops 2182086656 | bytes 9969664 | tf_op jit(solution)/shard_map/dot_general | solution.py:329
  166.1 2.4 %collective-permute-done.2 = bf16[256,1024]{1,0:T(8,128)(2,1)} collective-permute-done((bf16[256,1024]{1,0:T(8,128)(2,1)}, bf16[256,1024]{1,0:T(8,128)(2,1)}, u32[]{:S(2)}, u32[]{:S(2)}) %collective-permute-start.2) | collective-permute-done | bytes 524320 | tf_op jit(solution)/shard_map/ppermute | solution.py:368
  168.5 7.2 %convolution_convert_fusion.4 = bf16[128,1024]{1,0:T(8,128)(2,1)S(1)} fusion(bf16[2048,1024]{1,0:T(8,128)(2,1)} %param.19, bf16[1024,2048]{1,0:T(8,128)(2,1)} %param.17, f32[2048]{0:T(1024)S(1)} %copy-done.8, bf16[256,1024]{1,0:T(8,128)(2,1)} %collective-permute-done.2), kind=kOutput, calls=%fused_computation.30 | convolution fusion | flops 1091174400 | bytes 8921088 | tf_op jit(solution)/shard_map/dot_general | solution.py:329
  175.7 8.1 %convolution_convert_fusion.5 = bf16[128,1024]{1,0:T(8,128)(2,1)} fusion(bf16[2048,1024]{1,0:T(8,128)(2,1)} %param.19, bf16[1024,2048]{1,0:T(8,128)(2,1)} %param.17, f32[2048]{0:T(1024)S(1)} %copy-done.8, bf16[256,1024]{1,0:T(8,128)(2,1)} %collective-permute-done.2), kind=kOutput, calls=%fused_computation.31 | convolution fusion | flops 1091174400 | bytes 8921088 | tf_op jit(solution)/shard_map/dot_general | solution.py:329
  183.8 2.2 %collective-permute-start.3 = (bf16[128,1024]{1,0:T(8,128)(2,1)}, bf16[128,1024]{1,0:T(8,128)(2,1)S(1)}, u32[]{:S(2)}, u32[]{:S(2)}) collective-permute-start(bf16[128,1024]{1,0:T(8,128)(2,1)} %convolution_convert_fusion.5), channel_id=1, source_target_pairs={{0,1},{1,0},{2,3},{3,2},{4,5},{5,4},{6,7},{7,6},{8,9},{9,8},{10,11... | collective-permute-start | bytes 786440 | tf_op jit(solution)/shard_map/ppermute | solution.py:371
  186.1 0.1 collective-permute-start.4
  186.1 7.2 %collective-permute-done.3 = bf16[128,1024]{1,0:T(8,128)(2,1)S(1)} collective-permute-done((bf16[128,1024]{1,0:T(8,128)(2,1)}, bf16[128,1024]{1,0:T(8,128)(2,1)S(1)}, u32[]{:S(2)}, u32[]{:S(2)}) %collective-permute-start.3) | collective-permute-done | bytes 262176 | tf_op jit(solution)/shard_map/ppermute | solution.py:371
  193.4 5.1 %collective-permute-done.4 = bf16[128,1024]{1,0:T(8,128)(2,1)S(1)} collective-permute-done((bf16[128,1024]{1,0:T(8,128)(2,1)S(1)}, bf16[128,1024]{1,0:T(8,128)(2,1)S(1)}, u32[]{:S(2)}, u32[]{:S(2)}) %collective-permute-start.4) | collective-permute-done | bytes 262176 | tf_op jit(solution)/shard_map/ppermute | solution.py:371
  198.5 0.5 fusion.234
  199.0 0.3 multiply_reduce_fusion
  199.3 1.0 add_convert_fusion
  (22 shorter events, 0.1 us)
Async XLA Ops:
  0.0 136.3 %copy-start = (bf16[512,1024]{1,0:T(8,128)(2,1)S(1)}, bf16[512,1024]{1,0:T(8,128)(2,1)}, u32[]{:S(2)}) copy-start(bf16[512,1024]{1,0:T(8,128)(2,1)} %param.16) | copy-start | bytes 3145732
  0.0 15.1 %collective-permute-start = (bf16[256,1024]{1,0:T(8,128)(2,1)}, bf16[256,1024]{1,0:T(8,128)(2,1)S(1)}, u32[]{:S(2)}, u32[]{:S(2)}) collective-permute-start(bf16[256,1024]{1,0:T(8,128)(2,1)} %param.14), channel_id=1, source_target_pairs={{0,1},{1,0},{2,3},{3,2},{4,5},{5,4},{6,7},{7,6},{8,9},{9,8},{10,11... | collective-permute-start | bytes 1572872 | tf_op jit(solution)/shard_map/ppermute | solution.py:357
  2.9 15.3 %copy-start.1 = (bf16[256,1024]{1,0:T(8,128)(2,1)S(1)}, bf16[256,1024]{1,0:T(8,128)(2,1)}, u32[]{:S(2)}) copy-start(bf16[256,1024]{1,0:T(8,128)(2,1)} %param.14) | copy-start | bytes 1572868
  2.9 15.3 %copy-start.7 = (bf16[1024,3,512]{2,0,1:T(8,128)(2,1)S(1)}, bf16[1024,3,512]{2,0,1:T(8,128)(2,1)}, u32[]{:S(2)}) copy-start(bf16[1024,3,512]{2,0,1:T(8,128)(2,1)} %param.15) | copy-start | bytes 9437188
  137.7 13.2 %collective-permute-start.1 = (bf16[256,1024]{1,0:T(8,128)(2,1)S(1)}, bf16[256,1024]{1,0:T(8,128)(2,1)S(1)}, u32[]{:S(2)}, u32[]{:S(2)}) collective-permute-start(bf16[256,1024]{1,0:T(8,128)(2,1)S(1)} %convolution_convert_fusion), channel_id=1, source_target_pairs={{0,1},{1,0},{2,3},{3,2},{4,5},{5,4},{6,7},{7,6},{8,9},{9,8},{10,11... | collective-permute-start | bytes 1572872 | tf_op jit(solution)/shard_map/ppermute | solution.py:366
  139.5 13.2 %copy-start.2 = (f32[1024]{0:T(1024)S(1)}, f32[1024]{0:T(1024)}, u32[]{:S(2)}) copy-start(f32[1024]{0:T(1024)} %param.22) | copy-start | bytes 12292
  139.5 13.3 %copy-start.3 = (f32[1024]{0:T(1024)S(1)}, f32[1024]{0:T(1024)}, u32[]{:S(2)}) copy-start(f32[1024]{0:T(1024)} %param.21) | copy-start | bytes 12292
  152.5 3.4 %copy-start.8 = (f32[2048]{0:T(1024)S(1)}, f32[2048]{0:T(1024)}, u32[]{:S(2)}) copy-start(f32[2048]{0:T(1024)} %param.18) | copy-start | bytes 24580
  153.8 14.7 %collective-permute-start.2 = (bf16[256,1024]{1,0:T(8,128)(2,1)}, bf16[256,1024]{1,0:T(8,128)(2,1)}, u32[]{:S(2)}, u32[]{:S(2)}) collective-permute-start(bf16[256,1024]{1,0:T(8,128)(2,1)} %add_convert_fusion.1), channel_id=1, source_target_pairs={{0,1},{1,0},{2,3},{3,2},{4,5},{5,4},{6,7},{7,6},{8,9},{9,8},{10,11... | collective-permute-start | bytes 1572872 | tf_op jit(solution)/shard_map/ppermute | solution.py:368
  175.7 22.8 %copy-start.4 = (f32[1024]{0:T(1024)S(1)}, f32[1024]{0:T(1024)}, u32[]{:S(2)}) copy-start(f32[1024]{0:T(1024)} %param.20) | copy-start | bytes 12292
  183.8 15.4 %copy-start.5 = (f32[1024]{0:T(1024)S(1)}, f32[1024]{0:T(1024)}, u32[]{:S(2)}) copy-start(f32[1024]{0:T(1024)} %param.24) | copy-start | bytes 12292
  183.8 15.4 %copy-start.6 = (f32[1024]{0:T(1024)S(1)}, f32[1024]{0:T(1024)}, u32[]{:S(2)}) copy-start(f32[1024]{0:T(1024)} %param.23) | copy-start | bytes 12292
  183.8 9.5 %collective-permute-start.3 = (bf16[128,1024]{1,0:T(8,128)(2,1)}, bf16[128,1024]{1,0:T(8,128)(2,1)S(1)}, u32[]{:S(2)}, u32[]{:S(2)}) collective-permute-start(bf16[128,1024]{1,0:T(8,128)(2,1)} %convolution_convert_fusion.5), channel_id=1, source_target_pairs={{0,1},{1,0},{2,3},{3,2},{4,5},{5,4},{6,7},{7,6},{8,9},{9,8},{10,11... | collective-permute-start | bytes 786440 | tf_op jit(solution)/shard_map/ppermute | solution.py:371
  186.1 12.4 %collective-permute-start.4 = (bf16[128,1024]{1,0:T(8,128)(2,1)S(1)}, bf16[128,1024]{1,0:T(8,128)(2,1)S(1)}, u32[]{:S(2)}, u32[]{:S(2)}) collective-permute-start(bf16[128,1024]{1,0:T(8,128)(2,1)S(1)} %convolution_convert_fusion.4), channel_id=1, source_target_pairs={{0,1},{1,0},{2,3},{3,2},{4,5},{5,4},{6,7},{7,6},{8,9},{9,8},{10,11... | collective-permute-start | bytes 786440 | tf_op jit(solution)/shard_map/ppermute | solution.py:371
